TPU v7x, 32 devices: a whole 2x2x4 slice. The times are simulated.
32 devices in a mesh: mapx: 4 (over x, core), mapy: 4 (over z), layer: 2 (over y).
Axes of the slice: x: 2, y: 2, z: 4, core: 2. Of those that a mesh axis runs over, the one named last changes fastest.
Arguments:
- velocity: float32 [16, 2, 4, 32, 512], P(None, None, 'layer', 'mapx', 'mapy'), may hold values from -6 to 6
- viscosity: float32 [4, 32, 512], P('layer', 'mapx', 'mapy'), may hold values from 0.5 to 5
- friction: float32 [32, 512], P('mapx', 'mapy'), may hold values from 0.05 to 0.5
- owner: int32 [4, 4, 1024, 1], P('mapx', 'mapy'), may hold values from 0 to 7; in each aligned block of 1024 rows (0 to 1023, 1024 to 2047, ..., all dimensions but the last counted through in order) at most 256 rows name the same one
- cell: int32 [4, 4, 1024], P('mapx', 'mapy'), may hold values from 0 to 511
- directions: float32 [16, 16, 1024], P(None, 'mapx', ('mapy', 'layer')), may hold values from -6 to 6
- stiffness: float32 [16, 1024], P('mapx', ('mapy', 'layer')), may hold values from 0.02 to 0.2
Outputs:
- image: float32 [16, 2, 4, 32, 512], P(None, None, 'layer', 'mapx', 'mapy')
- hessian: float32 [16, 16, 1024], P(None, 'mapx', ('mapy', 'layer'))
Inputs may be any that keep to these rules, and one draw needn't show every extreme that they name: Among the faces of one mesh block (aligned blocks of 1024 rows) no owner is named more than 256 times, a bound that some block reaches.
All inputs are finite; a program needn't handle non-finite values.
Results may differ from a plain program's by a relative error of at most 0.00002.
Values sent between devices are 32-bit elements; how exact they have to be, the bound alone decides.
A program may use at most 64 MiB of HBM per device.

v0:
```python
import jax
import jax.numpy as jnp
from jax import lax
from jax.sharding import PartitionSpec as P


def with_halo(cells, sides, width):
    for axis, dim in sides:
        count = lax.axis_size(axis)
        ends = count - 1
        head = lax.slice_in_dim(cells, 0, width, axis=dim)
        tail = lax.slice_in_dim(cells, cells.shape[dim] - width, cells.shape[dim], axis=dim)
        cells = jnp.concatenate(
            [
                lax.ppermute(tail, axis, [(i, (i + 1) % count) for i in range(ends)]),
                cells,
                lax.ppermute(head, axis, [((i + 1) % count, i) for i in range(ends)]),
            ],
            axis=dim,
        )
    return cells


def broadcast(x, axis, root):
    mine = lax.axis_index(axis) == root
    return lax.psum(jnp.where(mine, x, jnp.zeros_like(x)), axis)


def stencil(padded, viscous):
    center = padded[..., 1:-1, 1:-1, 1:-1]
    visc = viscous[1:-1, 1:-1, 1:-1]
    weight_x = jnp.array([1.0, 0.25], jnp.float32)[:, None, None, None]
    weight_y = jnp.array([0.25, 1.0], jnp.float32)[:, None, None, None]
    total = 2.0 * 0.5 * (visc + viscous[2:, 1:-1, 1:-1]) * (center - padded[..., 2:, 1:-1, 1:-1])
    total = total + 2.0 * 0.5 * (visc + viscous[:-2, 1:-1, 1:-1]) * (
        center - padded[..., :-2, 1:-1, 1:-1]
    )
    total = total + weight_x * 0.5 * (visc + viscous[1:-1, 2:, 1:-1]) * (
        center - padded[..., 1:-1, 2:, 1:-1]
    )
    total = total + weight_x * 0.5 * (visc + viscous[1:-1, :-2, 1:-1]) * (
        center - padded[..., 1:-1, :-2, 1:-1]
    )
    total = total + weight_y * 0.5 * (visc + viscous[1:-1, 1:-1, 2:]) * (
        center - padded[..., 1:-1, 1:-1, 2:]
    )
    total = total + weight_y * 0.5 * (visc + viscous[1:-1, 1:-1, :-2]) * (
        center - padded[..., 1:-1, 1:-1, :-2]
    )
    return total


def laplace(padded):
    return (
        4.0 * padded[..., 1:-1, 1:-1]
        - padded[..., 2:, 1:-1]
        - padded[..., :-2, 1:-1]
        - padded[..., 1:-1, 2:]
        - padded[..., 1:-1, :-2]
    )


def map_border(field):
    return with_halo(field, (("mapx", 1), (("mapy", "layer"), 2)), 1)


def slot_places(keys, group_count, capacity, keep):
    onehot = (
        (keys[:, None] == jnp.arange(group_count, dtype=jnp.int32)[None, :]) & keep[:, None]
    ).astype(jnp.int32)
    before = jnp.cumsum(onehot, axis=0) - onehot
    slot_index = jnp.sum(before * onehot, axis=1)
    return jnp.where(keep, keys * capacity + slot_index, group_count * capacity)


def shards(velocity, viscosity, friction, owner, cell, directions, stiffness):
    probes = velocity.shape[0]
    depth, rows, cols = viscosity.shape
    stacked = jnp.concatenate([velocity.reshape(probes * 2, depth, rows, cols), viscosity[None]], 0)
    extended = with_halo(stacked, (("mapx", 2), ("mapy", 3), ("layer", 1)), 1)
    padded = extended[:-1].reshape(probes, 2, depth + 2, rows + 2, cols + 2)
    image = stencil(padded, extended[-1])
    face_count = rows * cols
    face_rows = (friction * (image[:, 0, 0] + image[:, 1, 0])).reshape(probes, face_count).T
    targets = owner.reshape(face_count)
    local_cells = cell.reshape(face_count).astype(jnp.float32)
    count_y = lax.axis_size("mapy")
    count_layer = lax.axis_size("layer")
    owner_count = count_y * count_layer
    capacity = 2 * face_count // owner_count
    my_layer = lax.axis_index("layer")
    spread = broadcast(face_rows, "layer", 0)
    keep = targets % count_layer == my_layer
    position = slot_places(targets // count_layer, count_y, capacity, keep)
    total_slots = count_y * capacity
    values = (
        jnp.zeros((total_slots + 1, probes), jnp.float32).at[position].set(spread)[:total_slots]
    )
    places = jnp.zeros((total_slots + 1,), jnp.float32).at[position].set(local_cells)[:total_slots]
    got_values, got_places = (
        lax.all_to_all(
            values.reshape(count_y, capacity, probes),
            "mapy",
            split_axis=0,
            concat_axis=0,
            tiled=True,
        ),
        lax.all_to_all(
            places.reshape(count_y, capacity), "mapy", split_axis=0, concat_axis=0, tiled=True
        ),
    )
    map_rows = directions.shape[1]
    map_cols = directions.shape[2]
    summed = jax.ops.segment_sum(
        got_values.reshape(-1, probes),
        got_places.reshape(-1).astype(jnp.int32),
        num_segments=map_rows * map_cols,
    )
    data = summed.T.reshape(probes, map_rows, map_cols)
    inner = stiffness[None] * laplace(map_border(directions))
    prior = laplace(map_border(inner))
    hessian = data + prior + 0.1 * directions
    return (image, hessian)


def solution(mesh):
    return jax.shard_map(
        shards,
        mesh=mesh,
        in_specs=(
            P(None, None, "layer", "mapx", "mapy"),
            P("layer", "mapx", "mapy"),
            P("mapx", "mapy"),
            P("mapx", "mapy", None, None),
            P("mapx", "mapy", None),
            P(None, "mapx", ("mapy", "layer")),
            P("mapx", ("mapy", "layer")),
        ),
        out_specs=(P(None, None, "layer", "mapx", "mapy"), P(None, "mapx", ("mapy", "layer"))),
        check_vma=False,
    )
```

profile of v0, /device:TPU:4, one launch (start us, length us, event | category | flops | bytes accessed | tf_op | source)
XLA Modules:
  0.0 132.0 jit_solution(15656060955295510216)
XLA Ops:
  10.0 1.1 reduce-window.6
  13.0 4.3 %scatter_custom_fusion = f32[1025]{0:T(1024)S(1)} fusion(s32[1024]{0:T(1024)S(1)} %bitcast.79, f32[1024]{0:T(1024)S(1)} %bitcast.82, f32[]{:T(128)} %constant.46.clone.1), kind=kCustom, calls=%fused_computation.105 | custom fusion | bytes 4104 | tf_op jit(solution)/shard_map/scatter | solution.py:99
  18.0 4.9 %all-to-all-start = ((f32[4,1,256]{2,1,0:T(1,128)}), f32[4,1,256]{2,1,0:T(1,128)S(1)}, u32[]{:S(2)}, u32[]{:S(2)}) async-start(f32[4,1,256]{2,1,0:T(1,128)} %bitcast.11), calls=%async_computation | async-start | bytes 8192 | tf_op jit(solution)/shard_map/all_to_all | solution.py:108
  23.7 1.3 collective-permute-start.6
  25.0 3.0 %collective-permute-start.7 = (f32[16,1,128]{2,1,0:T(1,128)S(1)}, f32[16,1,128]{2,1,0:T(1,128)S(1)}, u32[]{:S(2)}, u32[]{:S(2)}) collective-permute-start(f32[16,1,128]{2,1,0:T(1,128)S(1)} %get-tuple-element.22), channel_id=1, source_target_pairs={{0,8},{8,16},{16,24},{1,9},{9,17},{17,25},{2,10},{10,18},{18,26},{... | collective-permute-start | bytes 24584 | tf_op jit(solution)/shard_map/ppermute | solution.py:15
  29.1 3.0 %collective-permute-start = (f32[33,2,1,128]{3,2,1,0:T(1,128)S(1)}, f32[33,2,1,128]{3,2,1,0:T(1,128)S(1)}, u32[]{:S(2)}, u32[]{:S(2)}) collective-permute-start(f32[33,2,1,128]{3,2,1,0:T(1,128)S(1)} %get-tuple-element.8), channel_id=1, source_target_pairs={{0,8},{8,16},{16,24},{1,9},{9,17},{17,25},{2,10},{10,18},{18,26},{... | collective-permute-start | bytes 101384 | tf_op jit(solution)/shard_map/ppermute | solution.py:15
  32.2 1.3 collective-permute-start.1
  34.4 2.4 %collective-permute-start.8 = (f32[16,6,1]{2,1,0:T(8,128)S(1)}, f32[16,6,1]{2,1,0:T(8,128)S(1)}, u32[]{:S(2)}, u32[]{:S(2)}) collective-permute-start(f32[16,6,1]{2,1,0:T(8,128)S(1)} %get-tuple-element.12), channel_id=1, source_target_pairs={{1,0},{2,1},{3,2},{4,3},{5,4},{6,5},{7,6},{9,8},{10,9},{11,10},{12... | collective-permute-start | bytes 1160 | tf_op jit(solution)/shard_map/ppermute | solution.py:17
  36.8 4.3 %collective-permute-start.9 = (f32[16,6,1]{2,1,0:T(8,128)S(1)}, f32[16,6,1]{2,1,0:T(8,128)S(1)}, u32[]{:S(2)}, u32[]{:S(2)}) collective-permute-start(f32[16,6,1]{2,1,0:T(8,128)S(1)} %get-tuple-element.13), channel_id=1, source_target_pairs={{0,1},{1,2},{2,3},{3,4},{4,5},{5,6},{6,7},{8,9},{9,10},{10,11},{11... | collective-permute-start | bytes 1160 | tf_op jit(solution)/shard_map/ppermute | solution.py:15
  42.8 3.9 %collective-permute-start.2 = (f32[33,2,10,1]{0,1,3,2:T(2,128)S(1)}, f32[33,2,10,1]{0,1,3,2:T(2,128)S(1)}, u32[]{:S(2)}, u32[]{:S(2)}) collective-permute-start(f32[33,2,10,1]{0,1,3,2:T(2,128)S(1)} %copy.37), channel_id=1, source_target_pairs={{0,2},{2,4},{4,6},{1,3},{3,5},{5,7},{8,10},{10,12},{12,14},{9,11},... | collective-permute-start | bytes 7928 | tf_op jit(solution)/shard_map/ppermute | solution.py:15
  47.1 1.3 collective-permute-start.3
  49.2 3.4 %collective-permute-done.3 = f32[33,2,10,1]{0,1,3,2:T(2,128)S(1)} collective-permute-done((f32[33,2,10,1]{0,1,3,2:T(2,128)S(1)}, f32[33,2,10,1]{0,1,3,2:T(2,128)S(1)}, u32[]{:S(2)}, u32[]{:S(2)}) %collective-permute-start.3) | collective-permute-done | bytes 2672 | tf_op jit(solution)/shard_map/ppermute | solution.py:17
  54.5 1.3 collective-permute-start.4
  56.1 4.6 %collective-permute-start.5 = (f32[33,1,10,130]{3,1,2,0:T(1,128)S(1)}, f32[33,1,10,130]{3,1,2,0:T(1,128)S(1)}, u32[]{:S(2)}, u32[]{:S(2)}) collective-permute-start(f32[33,1,10,130]{3,1,2,0:T(1,128)S(1)} %copy.42), channel_id=1, source_target_pairs={{1,0},{3,2},{5,4},{7,6},{9,8},{11,10},{13,12},{15,14},{17,16},{19,... | collective-permute-start | bytes 514808 | tf_op jit(solution)/shard_map/ppermute | solution.py:17
  60.7 1.3 collective-permute-start.10
  62.0 3.2 %collective-permute-start.11 = (f32[16,1,128]{2,1,0:T(1,128)S(1)}, f32[16,1,128]{2,1,0:T(1,128)S(1)}, u32[]{:S(2)}, u32[]{:S(2)}) collective-permute-start(f32[16,1,128]{2,1,0:T(1,128)S(1)} %get-tuple-element.20), channel_id=1, source_target_pairs={{0,8},{8,16},{16,24},{1,9},{9,17},{17,25},{2,10},{10,18},{18,26},{... | collective-permute-start | bytes 24584 | tf_op jit(solution)/shard_map/ppermute | solution.py:15
  65.4 1.5 %collective-permute-done.5 = f32[33,1,10,130]{3,1,2,0:T(1,128)S(1)} collective-permute-done((f32[33,1,10,130]{3,1,2,0:T(1,128)S(1)}, f32[33,1,10,130]{3,1,2,0:T(1,128)S(1)}, u32[]{:S(2)}, u32[]{:S(2)}) %collective-permute-start.5) | collective-permute-done | bytes 171632 | tf_op jit(solution)/shard_map/ppermute | solution.py:17
  69.5 1.7 %fusion.4 = f32[16,2,2,8,128]{4,2,3,1,0:T(2,128)S(1)} fusion(f32[16,2,4,10,130]{4,2,3,1,0:T(4,128)S(1)} %bitcast.58, f32[2,2,8,128]{3,1,2,0:T(2,128)S(1)} %get-tuple-element.27, f32[2,2,8,128]{3,1,2,0:T(2,128)S(1)} %get-tuple-element.26, f32[2,2,8,128]{3,1,2,0:T(2,128)S(1)} %get-tuple-element.28, f32[2,2,8,128]{3,1,2,0:T(2,128)S(1)} %get-tuple-element.29, ...), kind=kLoop, calls=%fused_computation.12 | loop fusion | flops 1114112 | bytes 2179072 | tf_op jit(solution)/shard_map/add | solution.py:47
  72.6 27.4 %all-reduce.2.cloned.1.call-done = f32[1024,16]{1,0:T(8,128)} async-done(((f32[1024,16]{1,0:T(8,128)}), f32[1024,16]{1,0:T(8,128)}) %all-reduce.2.cloned.1.call-update) | async-done | bytes 65552 | tf_op jit(solution)/shard_map/psum | solution.py:26
  100.0 3.6 %scatter_custom_fusion.1 = f32[1025,16]{1,0:T(8,128)S(1)} fusion(s32[1024]{0:T(1024)S(1)} %bitcast.80, f32[1024,16]{1,0:T(8,128)} %all-reduce.2.cloned.1.call-done, f32[]{:T(128)} %constant.46.clone.1), kind=kCustom, calls=%fused_computation.8 | custom fusion | bytes 66112 | tf_op jit(solution)/shard_map/scatter | solution.py:97
  104.4 4.8 %all-to-all-start.1 = ((f32[4,256,16]{1,2,0:T(8,128)}), f32[4,256,16]{1,2,0:T(8,128)S(1)}, u32[]{:S(2)}, u32[]{:S(2)}) async-start(f32[4,256,16]{1,2,0:T(8,128)} %copy.48), calls=%async_computation.1 | async-start | bytes 131072 | tf_op jit(solution)/shard_map/all_to_all | solution.py:101
  109.3 3.4 %collective-permute-start.12 = (f32[16,6,1]{2,1,0:T(8,128)S(1)}, f32[16,6,1]{2,1,0:T(8,128)S(1)}, u32[]{:S(2)}, u32[]{:S(2)}) collective-permute-start(f32[16,6,1]{2,1,0:T(8,128)S(1)} %get-tuple-element.10), channel_id=1, source_target_pairs={{1,0},{2,1},{3,2},{4,3},{5,4},{6,5},{7,6},{9,8},{10,9},{11,10},{12... | collective-permute-start | bytes 1160 | tf_op jit(solution)/shard_map/ppermute | solution.py:17
  112.7 3.4 %collective-permute-start.13 = (f32[16,6,1]{2,1,0:T(8,128)S(1)}, f32[16,6,1]{2,1,0:T(8,128)S(1)}, u32[]{:S(2)}, u32[]{:S(2)}) collective-permute-start(f32[16,6,1]{2,1,0:T(8,128)S(1)} %get-tuple-element.11), channel_id=1, source_target_pairs={{0,1},{1,2},{2,3},{3,4},{4,5},{5,6},{6,7},{8,9},{9,10},{10,11},{11... | collective-permute-start | bytes 1160 | tf_op jit(solution)/shard_map/ppermute | solution.py:15
  117.0 7.3 %scatter_custom_fusion.2 = f32[512,16]{1,0:T(8,128)S(1)} fusion(s32[1024]{0:T(1024)S(1)} %bitcast.81, f32[1024,16]{1,0:T(8,128)S(1)} %bitcast.66, f32[]{:T(128)} %constant.46.clone.1), kind=kCustom, calls=%fused_computation.27 | custom fusion | flops 16384 | bytes 32772 | tf_op jit(solution)/shard_map/scatter-add | solution.py:114
  (79 shorter events, 19.8 us)
Async XLA Ops:
  18.0 15.5 %all-to-all-start = ((f32[4,1,256]{2,1,0:T(1,128)}), f32[4,1,256]{2,1,0:T(1,128)S(1)}, u32[]{:S(2)}, u32[]{:S(2)}) async-start(f32[4,1,256]{2,1,0:T(1,128)} %bitcast.11), calls=%async_computation | async-start | bytes 8192 | tf_op jit(solution)/shard_map/all_to_all | solution.py:108
  22.8 77.1 %all-reduce.2.cloned.1.call-start = ((), (), s32[]{:S(2)}) async-start(), calls=%async_computation.2 | async-start | bytes 1048576 | tf_op jit(solution)/shard_map/psum | solution.py:26
  23.7 9.8 %collective-permute-start.6 = (f32[16,1,128]{2,1,0:T(1,128)S(1)}, f32[16,1,128]{2,1,0:T(1,128)S(1)}, u32[]{:S(2)}, u32[]{:S(2)}) collective-permute-start(f32[16,1,128]{2,1,0:T(1,128)S(1)} %get-tuple-element.23), channel_id=1, source_target_pairs={{8,0},{16,8},{24,16},{9,1},{17,9},{25,17},{10,2},{18,10},{26,18},{... | collective-permute-start | bytes 24584 | tf_op jit(solution)/shard_map/ppermute | solution.py:17
  25.0 8.5 %collective-permute-start.7 = (f32[16,1,128]{2,1,0:T(1,128)S(1)}, f32[16,1,128]{2,1,0:T(1,128)S(1)}, u32[]{:S(2)}, u32[]{:S(2)}) collective-permute-start(f32[16,1,128]{2,1,0:T(1,128)S(1)} %get-tuple-element.22), channel_id=1, source_target_pairs={{0,8},{8,16},{16,24},{1,9},{9,17},{17,25},{2,10},{10,18},{18,26},{... | collective-permute-start | bytes 24584 | tf_op jit(solution)/shard_map/ppermute | solution.py:15
  29.1 12.0 %collective-permute-start = (f32[33,2,1,128]{3,2,1,0:T(1,128)S(1)}, f32[33,2,1,128]{3,2,1,0:T(1,128)S(1)}, u32[]{:S(2)}, u32[]{:S(2)}) collective-permute-start(f32[33,2,1,128]{3,2,1,0:T(1,128)S(1)} %get-tuple-element.8), channel_id=1, source_target_pairs={{0,8},{8,16},{16,24},{1,9},{9,17},{17,25},{2,10},{10,18},{18,26},{... | collective-permute-start | bytes 101384 | tf_op jit(solution)/shard_map/ppermute | solution.py:15
  32.2 9.0 %collective-permute-start.1 = (f32[33,2,1,128]{3,2,1,0:T(1,128)S(1)}, f32[33,2,1,128]{3,2,1,0:T(1,128)S(1)}, u32[]{:S(2)}, u32[]{:S(2)}) collective-permute-start(f32[33,2,1,128]{3,2,1,0:T(1,128)S(1)} %get-tuple-element.9), channel_id=1, source_target_pairs={{8,0},{16,8},{24,16},{9,1},{17,9},{25,17},{10,2},{18,10},{26,18},{... | collective-permute-start | bytes 101384 | tf_op jit(solution)/shard_map/ppermute | solution.py:17
  34.3 14.1 %copy-start.1 = (f32[16,4,128]{2,1,0:T(4,128)S(1)}, f32[16,4,128]{2,1,0:T(4,128)}, u32[]{:S(2)}) copy-start(f32[16,4,128]{2,1,0:T(4,128)} %param.14) | copy-start | bytes 98308
  34.3 14.1 %copy-start.4 = (f32[4,128]{1,0:T(4,128)S(1)}, f32[4,128]{1,0:T(4,128)}, u32[]{:S(2)}) copy-start(f32[4,128]{1,0:T(4,128)} %param.15) | copy-start | bytes 6148
  34.4 13.9 %collective-permute-start.8 = (f32[16,6,1]{2,1,0:T(8,128)S(1)}, f32[16,6,1]{2,1,0:T(8,128)S(1)}, u32[]{:S(2)}, u32[]{:S(2)}) collective-permute-start(f32[16,6,1]{2,1,0:T(8,128)S(1)} %get-tuple-element.12), channel_id=1, source_target_pairs={{1,0},{2,1},{3,2},{4,3},{5,4},{6,5},{7,6},{9,8},{10,9},{11,10},{12... | collective-permute-start | bytes 1160 | tf_op jit(solution)/shard_map/ppermute | solution.py:17
  36.8 11.5 %collective-permute-start.9 = (f32[16,6,1]{2,1,0:T(8,128)S(1)}, f32[16,6,1]{2,1,0:T(8,128)S(1)}, u32[]{:S(2)}, u32[]{:S(2)}) collective-permute-start(f32[16,6,1]{2,1,0:T(8,128)S(1)} %get-tuple-element.13), channel_id=1, source_target_pairs={{0,1},{1,2},{2,3},{3,4},{4,5},{5,6},{6,7},{8,9},{9,10},{10,11},{11... | collective-permute-start | bytes 1160 | tf_op jit(solution)/shard_map/ppermute | solution.py:15
  42.3 10.9 %copy-start = (f32[16,2,2,8,128]{4,3,2,1,0:T(8,128)S(1)}, f32[16,2,2,8,128]{4,3,2,1,0:T(8,128)}, u32[]{:S(2)}) copy-start(f32[16,2,2,8,128]{4,3,2,1,0:T(8,128)} %param.9) | copy-start | bytes 786436
  42.3 10.9 %copy-start.2 = (f32[2,8,128]{2,1,0:T(8,128)S(1)}, f32[2,8,128]{2,1,0:T(8,128)}, u32[]{:S(2)}) copy-start(f32[2,8,128]{2,1,0:T(8,128)} %param.10) | copy-start | bytes 24580
  42.8 5.8 %collective-permute-start.2 = (f32[33,2,10,1]{0,1,3,2:T(2,128)S(1)}, f32[33,2,10,1]{0,1,3,2:T(2,128)S(1)}, u32[]{:S(2)}, u32[]{:S(2)}) collective-permute-start(f32[33,2,10,1]{0,1,3,2:T(2,128)S(1)} %copy.37), channel_id=1, source_target_pairs={{0,2},{2,4},{4,6},{1,3},{3,5},{5,7},{8,10},{10,12},{12,14},{9,11},... | collective-permute-start | bytes 7928 | tf_op jit(solution)/shard_map/ppermute | solution.py:15
  47.1 5.6 %collective-permute-start.3 = (f32[33,2,10,1]{0,1,3,2:T(2,128)S(1)}, f32[33,2,10,1]{0,1,3,2:T(2,128)S(1)}, u32[]{:S(2)}, u32[]{:S(2)}) collective-permute-start(f32[33,2,10,1]{0,1,3,2:T(2,128)S(1)} %copy.38), channel_id=1, source_target_pairs={{2,0},{4,2},{6,4},{3,1},{5,3},{7,5},{10,8},{12,10},{14,12},{11,9},... | collective-permute-start | bytes 7928 | tf_op jit(solution)/shard_map/ppermute | solution.py:17
  54.5 10.9 %collective-permute-start.4 = (f32[33,1,10,130]{3,1,2,0:T(1,128)S(1)}, f32[33,1,10,130]{3,1,2,0:T(1,128)S(1)}, u32[]{:S(2)}, u32[]{:S(2)}) collective-permute-start(f32[33,1,10,130]{3,1,2,0:T(1,128)S(1)} %copy.41), channel_id=1, source_target_pairs={{0,1},{2,3},{4,5},{6,7},{8,9},{10,11},{12,13},{14,15},{16,17},{18,... | collective-permute-start | bytes 514808 | tf_op jit(solution)/shard_map/ppermute | solution.py:15
  56.1 10.8 %collective-permute-start.5 = (f32[33,1,10,130]{3,1,2,0:T(1,128)S(1)}, f32[33,1,10,130]{3,1,2,0:T(1,128)S(1)}, u32[]{:S(2)}, u32[]{:S(2)}) collective-permute-start(f32[33,1,10,130]{3,1,2,0:T(1,128)S(1)} %copy.42), channel_id=1, source_target_pairs={{1,0},{3,2},{5,4},{7,6},{9,8},{11,10},{13,12},{15,14},{17,16},{19,... | collective-permute-start | bytes 514808 | tf_op jit(solution)/shard_map/ppermute | solution.py:17
  60.7 11.8 %collective-permute-start.10 = (f32[16,1,128]{2,1,0:T(1,128)S(1)}, f32[16,1,128]{2,1,0:T(1,128)S(1)}, u32[]{:S(2)}, u32[]{:S(2)}) collective-permute-start(f32[16,1,128]{2,1,0:T(1,128)S(1)} %get-tuple-element.21), channel_id=1, source_target_pairs={{8,0},{16,8},{24,16},{9,1},{17,9},{25,17},{10,2},{18,10},{26,18},{... | collective-permute-start | bytes 24584 | tf_op jit(solution)/shard_map/ppermute | solution.py:17
  62.0 10.5 %collective-permute-start.11 = (f32[16,1,128]{2,1,0:T(1,128)S(1)}, f32[16,1,128]{2,1,0:T(1,128)S(1)}, u32[]{:S(2)}, u32[]{:S(2)}) collective-permute-start(f32[16,1,128]{2,1,0:T(1,128)S(1)} %get-tuple-element.20), channel_id=1, source_target_pairs={{0,8},{8,16},{16,24},{1,9},{9,17},{17,25},{2,10},{10,18},{18,26},{... | collective-permute-start | bytes 24584 | tf_op jit(solution)/shard_map/ppermute | solution.py:15
  68.1 1.3 %copy-start.5 = (f32[2]{0:T(128)S(1)}, f32[2]{0:T(128)}, u32[]{:S(2)}) copy-start(f32[2]{0:T(128)} %constant.61) | copy-start | bytes 28
  68.1 1.3 %copy-start.6 = (f32[2]{0:T(128)S(1)}, f32[2]{0:T(128)}, u32[]{:S(2)}) copy-start(f32[2]{0:T(128)} %constant.62) | copy-start | bytes 28
  69.4 2.1 %copy-start.3 = (f32[8,128]{1,0:T(8,128)S(1)}, f32[8,128]{1,0:T(8,128)}, u32[]{:S(2)}) copy-start(f32[8,128]{1,0:T(8,128)} %param.11) | copy-start | bytes 12292
  104.4 12.4 %all-to-all-start.1 = ((f32[4,256,16]{1,2,0:T(8,128)}), f32[4,256,16]{1,2,0:T(8,128)S(1)}, u32[]{:S(2)}, u32[]{:S(2)}) async-start(f32[4,256,16]{1,2,0:T(8,128)} %copy.48), calls=%async_computation.1 | async-start | bytes 131072 | tf_op jit(solution)/shard_map/all_to_all | solution.py:101
  109.3 15.1 %collective-permute-start.12 = (f32[16,6,1]{2,1,0:T(8,128)S(1)}, f32[16,6,1]{2,1,0:T(8,128)S(1)}, u32[]{:S(2)}, u32[]{:S(2)}) collective-permute-start(f32[16,6,1]{2,1,0:T(8,128)S(1)} %get-tuple-element.10), channel_id=1, source_target_pairs={{1,0},{2,1},{3,2},{4,3},{5,4},{6,5},{7,6},{9,8},{10,9},{11,10},{12... | collective-permute-start | bytes 1160 | tf_op jit(solution)/shard_map/ppermute | solution.py:17
  112.7 11.7 %collective-permute-start.13 = (f32[16,6,1]{2,1,0:T(8,128)S(1)}, f32[16,6,1]{2,1,0:T(8,128)S(1)}, u32[]{:S(2)}, u32[]{:S(2)}) collective-permute-start(f32[16,6,1]{2,1,0:T(8,128)S(1)} %get-tuple-element.11), channel_id=1, source_target_pairs={{0,1},{1,2},{2,3},{3,4},{4,5},{5,6},{6,7},{8,9},{9,10},{10,11},{11... | collective-permute-start | bytes 1160 | tf_op jit(solution)/shard_map/ppermute | solution.py:15
Sparse Core Ops, SparseCore 0:
  72.7 27.2 all-reduce.1
where the time goes:
time: 134 us; the launch traced here: 132 us
  starting transfers between devices  47.4 us (35%)
  waiting for transfers between devices  32.4 us (24%)
  other arithmetic  21.5 us (16%)
  local copies, waits for them, and re-layouts  16.1 us (12%)
  between operations  14.6 us (11%)
    psum x1, waiting for transfers between devices, broadcast(): return lax.psum(jnp.where(mine, x, jnp.zeros_like(x)), axis)  27.4 us
    ppermute x7, starting transfers between devices, with_halo(): lax.ppermute(tail, axis, [(i, (i + 1) % count) for i in range(ends)])  22.2 us
    ppermute x7, starting transfers between devices, with_halo(): lax.ppermute(head, axis, [((i + 1) % count, i) for i in range(ends)])  15.5 us
    scatter-add x1, other arithmetic, shards(): jax.ops.segment_sum(got_values.reshape(-1, probes), got_places.reshape(-1...  7.26 us
    ppermute x7, waiting for transfers between devices, with_halo(): lax.ppermute(head, axis, [((i + 1) % count, i) for i in range(ends)])  4.94 us
    all_to_all x1, starting transfers between devices, shards(): lax.all_to_all(places.reshape(count_y, capacity), 'mapy', split_axis=0, c...  4.87 us
    all_to_all x1, starting transfers between devices, shards(): lax.all_to_all(values.reshape(count_y, capacity, probes), 'mapy', split_a...  4.84 us
    scatter x1, local copies, waits for them, and re-layouts, shards(): jnp.zeros((total_slots + 1,), jnp.float32).at[position].set(local_cells)  4.31 us
  transfers between devices with their start and end apart: 17, of which 4 were waited for; matrix products, arithmetic and copies ran while one was open for 15% of the time, Pallas kernels for 0%

commit v1 on v0

v1 whole, which is shorter than its diff:
```python
import functools

import jax
import jax.numpy as jnp
from jax import lax
from jax.experimental import pallas as pl
from jax.experimental.pallas import tpu as pltpu
from jax.sharding import PartitionSpec as P

F32 = jnp.float32
BF16 = jnp.bfloat16
X, Y, ZV, ZM, R, C = 0, 2, 4, 6, 8, 10


def corner_slot(dx, do):
    return (dx + 1) * 2 + (0 if do < 0 else 1)


def kernel(
    counts, vel, visc, fric, own, cell, dirs, stiff, img, hess,
    xs, xh, ys, yh, zh, mh, cs, ch, rs, rh, tr, onehot, lhs, part, got, prior,
    send, recv, part_send, part_recv,
):
    nx, ny, nl = counts
    no = ny * nl
    nq, depth, rows, cols = vel.shape
    nv = nq * depth
    probes = nq // 2
    mrows, mcols = stiff.shape
    halves = probes // 8
    ix, iy, il = lax.axis_index("mapx"), lax.axis_index("mapy"), lax.axis_index("layer")
    me = iy * nl + il

    def place(at_x, owner):
        return (at_x, lax.div(owner, nl), lax.rem(owner, nl))

    low_x, high_x = ix > 0, ix < nx - 1
    low_y, high_y = iy > 0, iy < ny - 1
    low_l, high_l = il > 0, il < nl - 1
    low_o, high_o = me > 0, me < no - 1

    def has(dx, do):
        good_x = {-1: low_x, 1: high_x}.get(dx)
        good_o = {-1: low_o, 1: high_o}.get(do)
        if good_x is None:
            return good_o
        return good_x if good_o is None else jnp.logical_and(good_x, good_o)

    barrier = pltpu.get_barrier_semaphore()
    for step in range(1, no):
        other = lax.rem(me + step, no)
        pl.semaphore_signal(
            barrier, inc=1, device_id=place(ix, other), device_id_type=pl.DeviceIdType.MESH
        )
    greeted = no - 1
    for dx in (-1, 1):
        for do in (-1, 0, 1):
            near = has(dx, do)
            greeted = greeted + near.astype(jnp.int32)

            @pl.when(near)
            def _(dx=dx, do=do):
                pl.semaphore_signal(
                    barrier, inc=1, device_id=place(ix + dx, me + do),
                    device_id_type=pl.DeviceIdType.MESH,
                )

    def remote(src, dst, out_sem, in_sem, device):
        return pltpu.make_async_remote_copy(
            src_ref=src, dst_ref=dst, send_sem=out_sem, recv_sem=in_sem,
            device_id=device, device_id_type=pl.DeviceIdType.MESH,
        )

    def pair(kind, src, dst, side, device):
        return remote(src, dst, send.at[kind + side], recv.at[kind + 1 - side], device)

    def x_copy(side):
        return pair(X, xs.at[side], xh.at[1 - side], side, place(ix + 2 * side - 1, me))

    def r_copy(side):
        return pair(R, rs.at[side], rh.at[1 - side], side, place(ix + 2 * side - 1, me))

    def y_copy(side):
        return pair(Y, ys.at[side], yh.at[1 - side], side, (ix, iy + 2 * side - 1, il))

    def z_copy(side):
        z = 0 if side == 0 else depth - 1
        return pair(ZV, vel.at[:, z], zh.at[1 - side], side, (ix, iy, il + 2 * side - 1))

    def m_copy(side):
        z = 0 if side == 0 else depth - 1
        return pair(ZM, visc.at[z], mh.at[1 - side], side, (ix, iy, il + 2 * side - 1))

    def c_copy(dx, do):
        return remote(
            cs.at[0 if do < 0 else 1], ch.at[corner_slot(-dx, -do)],
            send.at[C + corner_slot(dx, do)], recv.at[C + corner_slot(-dx, -do)],
            place(ix + dx, me + do),
        )

    lane = lax.broadcasted_iota(jnp.int32, (rows, cols), 1)
    sub = lax.broadcasted_iota(jnp.int32, (rows, cols), 0)
    zeros = jnp.zeros((rows, cols), F32)

    for z in range(depth):
        xs[0, z * nq:(z + 1) * nq, :] = vel[:, z, 0, :]
        xs[1, z * nq:(z + 1) * nq, :] = vel[:, z, rows - 1, :]
    for side, row in ((0, 0), (1, rows - 1)):
        xs[side, nv:nv + 8, :] = jnp.concatenate(
            [visc[z, row:row + 1, :] for z in range(depth)]
            + [jnp.zeros((8 - depth, cols), F32)], 0,
        )

    def put(value, at, packed):
        here = lane == at
        return (
            jnp.where(here, pltpu.roll(value, at, 1), packed[0]),
            jnp.where(here, pltpu.roll(value, at + 1, 1), packed[1]),
        )

    def pack_y(q, packed):
        for z in range(depth):
            packed = put(vel[q, z], z * nq + q, packed)
        return packed

    packed = lax.fori_loop(0, nq, pack_y, (zeros, zeros), unroll=8)
    for z in range(depth):
        packed = put(visc[z], nv + z, packed)
    ys[0], ys[1] = packed

    block = [dirs[pl.ds(r, probes, stride=mrows), :] for r in range(mrows)]
    rim = jnp.concatenate([stiff[...], jnp.zeros((8 - mrows, mcols), F32)], 0)
    for side, first in ((0, 0), (1, mrows - 2)):
        for r in range(2):
            rs[side, r * probes:(r + 1) * probes, :] = block[first + r]
        rs[side, 2 * probes:2 * probes + 8, :] = rim
        cs[side, 8:16, :] = rim
    two = lax.div(lane, 2)
    packed = (zeros, zeros)
    for k in range(mrows * halves):
        value = block[k // halves][(k % halves) * 8:(k % halves) * 8 + 8]
        packed = (
            jnp.where(two == k, pltpu.roll(value, 2 * k, 1) if k else value, packed[0]),
            jnp.where(two == k, pltpu.roll(value, 2 * k + 2, 1), packed[1]),
        )
    cs[0, 0:8, :], cs[1, 0:8, :] = packed

    pl.semaphore_wait(barrier, greeted)

    def when_near(near, copy):
        @pl.when(near)
        def _():
            copy().start()

    sides = (0, 1)
    near_x, near_y, near_l = (low_x, high_x), (low_y, high_y), (low_l, high_l)
    corners = [(dx, do) for dx in (-1, 0, 1) for do in (-1, 1)]
    for s in sides:
        when_near(near_x[s], functools.partial(x_copy, s))
        when_near(near_y[s], functools.partial(y_copy, s))
    for s in sides:
        when_near(near_l[s], functools.partial(m_copy, s))
        when_near(near_l[s], functools.partial(z_copy, s))
    for s in sides:
        when_near(near_x[s], functools.partial(r_copy, s))
    for dx, do in corners:
        when_near(has(dx, do), functools.partial(c_copy, dx, do))

    def zero_unless(near, ref, at):
        @pl.when(jnp.logical_not(near))
        def _():
            ref[at] = jnp.zeros(ref.shape[1:], F32)

    for s in sides:
        zero_unless(near_x[s], xh, s)
        zero_unless(near_y[s], yh, s)
        zero_unless(near_l[s], zh, s)
        zero_unless(near_l[s], mh, s)
        zero_unless(near_x[s], rh, s)
    for dx, do in corners:
        zero_unless(has(dx, do), ch, corner_slot(dx, do))

    span = 2 * mcols
    pairs = mrows // 2
    cells = cell[...]
    low = lax.rem(cells, span)
    group = own[...] * pairs + lax.div(cells, span)
    number = lax.broadcasted_iota(jnp.int32, (span, cols), 0)
    for x in range(rows):
        onehot[:, x * cols:(x + 1) * cols] = jnp.where(
            number == low[x:x + 1, :], 1.0, 0.0
        ).astype(BF16)

    def arrive(near, copy):
        @pl.when(near)
        def _():
            copy().wait_recv()

    def beside(value, index, halo_rows, halo_lanes):
        down = jnp.where(sub == 0, halo_rows[0], pltpu.roll(value, 1, 0))
        up = jnp.where(sub == rows - 1, halo_rows[1], pltpu.roll(value, rows - 1, 0))
        left = jnp.where(
            lane == 0, pltpu.roll(halo_lanes[0], cols - index, 1), pltpu.roll(value, 1, 1)
        )
        right = jnp.where(
            lane == cols - 1,
            pltpu.roll(halo_lanes[1], cols - 1 - index, 1),
            pltpu.roll(value, cols - 1, 1),
        )
        return down, up, left, right

    def rows_at(index):
        return tuple(
            jnp.broadcast_to(xh[s, pl.ds(index, 1), :], (rows, cols)) for s in sides
        )

    def plane(z, trace):
        lanes = (yh[0], yh[1])
        here = visc[z]
        around = beside(here, nv + z, rows_at(nv + z), lanes)
        mean = [0.5 * (here + other) for other in around]
        down_z = here + (mh[0] if z == 0 else visc[z - 1])
        up_z = here + (mh[1] if z == depth - 1 else visc[z + 1])
        weights = (
            (mean[0], mean[1], 0.25 * mean[2], 0.25 * mean[3]),
            (0.25 * mean[0], 0.25 * mean[1], mean[2], mean[3]),
        )
        rub = fric[...]

        def probe(p, carry):
            both = None
            for c in range(2):
                q = p * 2 + c
                value = vel[q, z]
                below = zh[0, q] if z == 0 else vel[q, z - 1]
                above = zh[1, q] if z == depth - 1 else vel[q, z + 1]
                index = z * nq + q
                total = up_z * (value - above) + down_z * (value - below)
                for weight, other in zip(
                    weights[c], beside(value, index, rows_at(index), lanes)
                ):
                    total = total + weight * (value - other)
                img[q, z] = total
                both = total if both is None else both + total
            if trace:
                tr[pl.ds(p, rows, stride=probes), :] = rub * both
            return carry

        lax.fori_loop(0, probes, probe, 0, unroll=4)

    for s in sides:
        arrive(near_x[s], functools.partial(x_copy, 1 - s))
        arrive(near_y[s], functools.partial(y_copy, 1 - s))

    chunk = min(8, no)
    tall = 2 * probes

    def part_copy(owner):
        return remote(
            part.at[owner], got.at[iy], part_send.at[owner], part_recv.at[iy], place(ix, owner)
        )

    @pl.when(il == 0)
    def _():
        plane(0, True)
        coarse, fine = [], []
        for x in range(rows):
            values = tr[x * probes:(x + 1) * probes, :]
            coarse.append(values.astype(BF16).astype(F32))
            fine.append(values - coarse[-1])

        def owners(base):
            for g in range(chunk * pairs):
                for x in range(rows):
                    mine = group[x:x + 1, :] == base * pairs + g
                    lhs[g * tall:(g + 1) * tall, x * cols:(x + 1) * cols] = jnp.concatenate(
                        [jnp.where(mine, coarse[x], 0.0), jnp.where(mine, fine[x], 0.0)], 0
                    ).astype(BF16)
            sums = lax.dot_general(
                lhs[...], onehot[...], (((1,), (1,)), ((), ())), preferred_element_type=F32
            )
            for j in range(chunk):
                for h in range(pairs):
                    at = (j * pairs + h) * tall
                    both = sums[at:at + probes] + sums[at + probes:at + tall]
                    for k in range(2):
                        row = (2 * h + k) * probes
                        part[base + j, row:row + probes, :] = both[:, k * mcols:(k + 1) * mcols]
            for j in range(chunk):
                @pl.when(base + j != me)
                def _(j=j):
                    part_copy(base + j).start()

        if no == chunk:
            owners(0)
        else:
            def step(i, carry):
                owners(i * chunk)
                return carry

            lax.fori_loop(0, no // chunk, step, 0)

    for s in sides:
        arrive(near_x[s], functools.partial(r_copy, 1 - s))
    for dx, do in corners:
        arrive(has(dx, do), functools.partial(c_copy, -dx, -do))

    def edge(dx, r):
        left, right = ch[corner_slot(dx, -1), 0:8, :], ch[corner_slot(dx, 1), 0:8, :]
        halfs = []
        for h in range(halves):
            k = 2 * (r * halves + h)
            from_right = pltpu.roll(right, mcols - k, 1) if k else right
            from_left = pltpu.roll(left, mcols - 2 - k, 1)
            halfs.append(
                jnp.where(lane < 2, from_right, jnp.where(lane >= mcols - 2, from_left, 0.0))
            )
        return jnp.concatenate(halfs, 0)

    wide = {}
    for r in range(2):
        wide[r - 2] = jnp.concatenate(
            [rh[0, r * probes:(r + 1) * probes, :], edge(-1, mrows - 2 + r)], 1
        )
        wide[mrows + r] = jnp.concatenate(
            [rh[1, r * probes:(r + 1) * probes, :], edge(1, r)], 1
        )
    for r in range(mrows):
        wide[r] = jnp.concatenate([dirs[pl.ds(r, probes, stride=mrows), :], edge(0, r)], 1)

    def laplace(field, r):
        return (
            4.0 * field[r] - field[r - 1] - field[r + 1]
            - pltpu.roll(field[r], 1, 1) - pltpu.roll(field[r], 2 * mcols - 1, 1)
        )

    line = lax.broadcasted_iota(jnp.int32, (1, mcols), 1)
    inner = {}
    for r in range(-1, mrows + 1):
        if r < 0:
            soft = rh[0, 2 * probes + mrows - 1:2 * probes + mrows, :]
        elif r == mrows:
            soft = rh[1, 2 * probes:2 * probes + 1, :]
        else:
            soft = stiff[r:r + 1, :]
        outer = jnp.zeros((1, mcols), F32)
        if 0 <= r < mrows:
            outer = jnp.where(
                line == 0, ch[corner_slot(0, 1), 8 + r:9 + r, :],
                jnp.where(line == mcols - 1, ch[corner_slot(0, -1), 8 + r:9 + r, :], 0.0),
            )
        inner[r] = jnp.concatenate([soft, outer], 1) * laplace(wide, r)
    for r in range(mrows):
        prior[r * probes:(r + 1) * probes, :] = (
            laplace(inner, r) + 0.1 * wide[r]
        )[:, :mcols]

    for s in sides:
        arrive(near_l[s], functools.partial(m_copy, 1 - s))
        arrive(near_l[s], functools.partial(z_copy, 1 - s))

    @pl.when(il != 0)
    def _():
        plane(0, False)

    for z in range(1, depth):
        plane(z, False)

    for b in range(ny):
        at_home = jnp.logical_and(il == 0, iy == b)

        @pl.when(at_home)
        def _():
            prior[...] += part[me]

        @pl.when(jnp.logical_not(at_home))
        def _(b=b):
            remote(
                part.at[0], got.at[b], part_send.at[0], part_recv.at[b], place(ix, me)
            ).wait_recv()
            prior[...] += got[b]

    for r in range(mrows):
        hess[pl.ds(r, probes, stride=mrows), :] = prior[r * probes:(r + 1) * probes, :]

    def sent(near, copy):
        @pl.when(near)
        def _():
            copy().wait_send()

    for s in sides:
        for near, copy in (
            (near_x[s], x_copy), (near_y[s], y_copy), (near_l[s], m_copy),
            (near_l[s], z_copy), (near_x[s], r_copy),
        ):
            sent(near, functools.partial(copy, s))
    for dx, do in corners:
        sent(has(dx, do), functools.partial(c_copy, dx, do))
    for owner in range(no):
        sent(jnp.logical_and(il == 0, me != owner), functools.partial(part_copy, owner))


def shards(velocity, viscosity, friction, owner, cell, directions, stiffness):
    probes = velocity.shape[0]
    depth, rows, cols = viscosity.shape
    mrows, mcols = stiffness.shape
    counts = tuple(lax.axis_size(axis) for axis in ("mapx", "mapy", "layer"))
    no = counts[1] * counts[2]
    nq = probes * 2
    nv = nq * depth
    chunk = min(8, no)
    vmem = pl.BlockSpec(memory_space=pltpu.VMEM)
    image, hessian = pl.pallas_call(
        functools.partial(kernel, counts),
        out_shape=(
            jax.ShapeDtypeStruct((nq, depth, rows, cols), F32),
            jax.ShapeDtypeStruct((probes * mrows, mcols), F32),
        ),
        in_specs=[vmem] * 7,
        out_specs=(vmem, vmem),
        scratch_shapes=[
            pltpu.VMEM((2, nv + 8, cols), F32),
            pltpu.VMEM((2, nv + 8, cols), F32),
            pltpu.VMEM((2, rows, cols), F32),
            pltpu.VMEM((2, rows, cols), F32),
            pltpu.VMEM((2, nq, rows, cols), F32),
            pltpu.VMEM((2, rows, cols), F32),
            pltpu.VMEM((2, 16, mcols), F32),
            pltpu.VMEM((6, 16, mcols), F32),
            pltpu.VMEM((2, 2 * probes + 8, mcols), F32),
            pltpu.VMEM((2, 2 * probes + 8, mcols), F32),
            pltpu.VMEM((rows * probes, cols), F32),
            pltpu.VMEM((2 * mcols, rows * cols), BF16),
            pltpu.VMEM((chunk * (mrows // 2) * 2 * probes, rows * cols), BF16),
            pltpu.VMEM((no, mrows * probes, mcols), F32),
            pltpu.VMEM((counts[1], mrows * probes, mcols), F32),
            pltpu.VMEM((mrows * probes, mcols), F32),
            pltpu.SemaphoreType.DMA((16,)),
            pltpu.SemaphoreType.DMA((16,)),
            pltpu.SemaphoreType.DMA((no,)),
            pltpu.SemaphoreType.DMA((counts[1],)),
        ],
        compiler_params=pltpu.CompilerParams(
            collective_id=0, has_side_effects=True, vmem_limit_bytes=32 << 20
        ),
        name="hessian_action",
    )(
        velocity.reshape(nq, depth, rows, cols),
        viscosity,
        friction,
        owner.reshape(rows, cols),
        cell.reshape(rows, cols),
        directions.reshape(probes * mrows, mcols),
        stiffness,
    )
    return image.reshape(velocity.shape), hessian.reshape(directions.shape)


def solution(mesh):
    return jax.shard_map(
        shards,
        mesh=mesh,
        in_specs=(
            P(None, None, "layer", "mapx", "mapy"),
            P("layer", "mapx", "mapy"),
            P("mapx", "mapy"),
            P("mapx", "mapy", None, None),
            P("mapx", "mapy", None),
            P(None, "mapx", ("mapy", "layer")),
            P("mapx", ("mapy", "layer")),
        ),
        out_specs=(P(None, None, "layer", "mapx", "mapy"), P(None, "mapx", ("mapy", "layer"))),
        check_vma=False,
    )
```

time: 134 us -> 22.8 us (0.17)
  the two profiles are of different devices: /device:TPU:4 before, /device:TPU:0 now
where the time goes in v1:
time: 22.8 us; the launch traced here: 22.4 us
  Pallas kernels  16 us (70%)
  local copies, waits for them, and re-layouts  5.78 us (25%)
  between operations  0.66 us (3%)
    pallas_call x1, Pallas kernels, shards(): pl.pallas_call(functools.partial(kernel, counts), out_shape=(jax.ShapeDty...  16 us
    unnamed x16, local copies, waits for them, and re-layouts  5.78 us

profile of v1, /device:TPU:0, one launch (start us, length us, event | category | flops | bytes accessed | tf_op | source)
XLA Modules:
  0.0 22.4 jit_solution(1479281634722274301)
XLA Ops:
  0.6 0.0 copy-start.3
  0.6 0.0 copy-start.6
  0.7 0.7 %copy-done.3 = f32[8,128]{1,0:T(8,128)S(1)} copy-done((f32[8,128]{1,0:T(8,128)S(1)}, f32[8,128]{1,0:T(8,128)}, u32[]{:S(2)}) %copy-start.3) | copy-done | bytes 4120
  1.3 0.0 copy-done.6
  1.3 0.0 copy-start
  1.3 0.9 %copy-done = f32[16,2,2,8,128]{4,3,2,1,0:T(8,128)S(1)} copy-done((f32[16,2,2,8,128]{4,3,2,1,0:T(8,128)S(1)}, f32[16,2,2,8,128]{4,3,2,1,0:T(8,128)}, u32[]{:S(2)}) %copy-start) | copy-done | bytes 262168
  2.3 0.0 copy-start.1
  2.3 0.8 %copy-done.1 = f32[16,4,128]{2,1,0:T(4,128)S(1)} copy-done((f32[16,4,128]{2,1,0:T(4,128)S(1)}, f32[16,4,128]{2,1,0:T(4,128)}, u32[]{:S(2)}) %copy-start.1) | copy-done | bytes 32792
  3.0 0.0 copy-start.2
  3.0 0.7 %copy-done.2 = f32[2,8,128]{2,1,0:T(8,128)S(1)} copy-done((f32[2,8,128]{2,1,0:T(8,128)S(1)}, f32[2,8,128]{2,1,0:T(8,128)}, u32[]{:S(2)}) %copy-start.2) | copy-done | bytes 8216
  3.7 0.0 copy-start.4
  3.7 0.7 %copy-done.4 = s32[1,1,1024,1]{2,3,1,0:T(1,128)S(1)} copy-done((s32[1,1,1024,1]{2,3,1,0:T(1,128)S(1)}, s32[1,1,1024,1]{2,3,1,0:T(1,128)}, u32[]{:S(2)}) %copy-start.4) | copy-done | bytes 4120
  4.4 0.0 copy-start.5
  4.4 0.7 %copy-done.5 = s32[1,1,1024]{2,1,0:T(1,128)S(1)} copy-done((s32[1,1,1024]{2,1,0:T(1,128)S(1)}, s32[1,1,1024]{2,1,0:T(1,128)}, u32[]{:S(2)}) %copy-start.5) | copy-done | bytes 4120
  5.1 16.0 %hessian_action.1 = (f32[32,2,8,128]{3,2,1,0:T(8,128)S(1)}, f32[64,128]{1,0:T(8,128)S(1)}) custom-call(f32[32,2,8,128]{3,2,1,0:T(8,128)S(1)} %bitcast.6, f32[2,8,128]{2,1,0:T(8,128)S(1)} %copy-done.2, f32[8,128]{1,0:T(8,128)S(1)} %copy-done.3, s32[8,128]{1,0:T(8,128)S(1)} %bitcast.10, s32[8,128]{1,0:T(8,128)S(1)} %bitcast.11, f32[64,128]{1,0:T(8,128)S(1)} %bitcast.8, ...), custom_call_target="tpu_custom_call" | custom-call | tf_op jit(solution)/shard_map/hessian_action/pallas_call | solution.py:413
  21.1 0.7 %copy.11 = f32[16,2,2,8,128]{4,3,2,1,0:T(8,128)} copy(f32[16,2,2,8,128]{4,3,2,1,0:T(8,128)S(1)} %bitcast.7) | data formatting | bytes 524288
  21.8 0.6 %copy.12 = f32[16,4,128]{2,1,0:T(4,128)} copy(f32[16,4,128]{2,1,0:T(4,128)S(1)} %bitcast.9) | data formatting | bytes 65536
Async XLA Ops:
  0.6 0.7 %copy-start.3 = (f32[8,128]{1,0:T(8,128)S(1)}, f32[8,128]{1,0:T(8,128)}, u32[]{:S(2)}) copy-start(f32[8,128]{1,0:T(8,128)} %fric.1) | copy-start | bytes 12292
  0.6 0.7 %copy-start.6 = (f32[4,128]{1,0:T(4,128)S(1)}, f32[4,128]{1,0:T(4,128)}, u32[]{:S(2)}) copy-start(f32[4,128]{1,0:T(4,128)} %stiff.1) | copy-start | bytes 6148
  1.3 0.9 %copy-start = (f32[16,2,2,8,128]{4,3,2,1,0:T(8,128)S(1)}, f32[16,2,2,8,128]{4,3,2,1,0:T(8,128)}, u32[]{:S(2)}) copy-start(f32[16,2,2,8,128]{4,3,2,1,0:T(8,128)} %param.7) | copy-start | bytes 786436
  2.3 0.8 %copy-start.1 = (f32[16,4,128]{2,1,0:T(4,128)S(1)}, f32[16,4,128]{2,1,0:T(4,128)}, u32[]{:S(2)}) copy-start(f32[16,4,128]{2,1,0:T(4,128)} %param.12) | copy-start | bytes 98308
  3.0 0.7 %copy-start.2 = (f32[2,8,128]{2,1,0:T(8,128)S(1)}, f32[2,8,128]{2,1,0:T(8,128)}, u32[]{:S(2)}) copy-start(f32[2,8,128]{2,1,0:T(8,128)} %visc.1) | copy-start | bytes 24580
  3.7 0.7 %copy-start.4 = (s32[1,1,1024,1]{2,3,1,0:T(1,128)S(1)}, s32[1,1,1024,1]{2,3,1,0:T(1,128)}, u32[]{:S(2)}) copy-start(s32[1,1,1024,1]{2,3,1,0:T(1,128)} %param.10) | copy-start | bytes 12292
  4.4 0.7 %copy-start.5 = (s32[1,1,1024]{2,1,0:T(1,128)S(1)}, s32[1,1,1024]{2,1,0:T(1,128)}, u32[]{:S(2)}) copy-start(s32[1,1,1024]{2,1,0:T(1,128)} %param.11) | copy-start | bytes 12292

commit v2 on v1

--- a/solution.py
+++ b/solution.py
@@ -17,10 +17,20 @@
 
 
 def kernel(
-    counts, vel, visc, fric, own, cell, dirs, stiff, img, hess,
-    xs, xh, ys, yh, zh, mh, cs, ch, rs, rh, tr, onehot, lhs, part, got, prior,
-    send, recv, part_send, part_recv,
+    counts, *refs,
 ):
+    inputs, (img_out, hess_out), staged, (img, hess) = refs[:7], refs[7:9], refs[9:16], refs[16:18]
+    (
+        xs, xh, ys, yh, zh, mh, cs, ch, rs, rh, tr, onehot, lhs, part, got, prior,
+        load, store, send, recv, part_send, part_recv, trace_send, trace_recv,
+    ) = refs[18:]
+    loads = [
+        pltpu.make_async_copy(src, dst, load.at[i])
+        for i, (src, dst) in enumerate(zip(inputs, staged))
+    ]
+    for copy in loads:
+        copy.start()
+    vel, visc, fric, own, cell, dirs, stiff = staged
     nx, ny, nl = counts
     no = ny * nl
     nq, depth, rows, cols = vel.shape
@@ -102,6 +112,8 @@
     sub = lax.broadcasted_iota(jnp.int32, (rows, cols), 0)
     zeros = jnp.zeros((rows, cols), F32)
 
+    loads[0].wait()
+    loads[1].wait()
     for z in range(depth):
         xs[0, z * nq:(z + 1) * nq, :] = vel[:, z, 0, :]
         xs[1, z * nq:(z + 1) * nq, :] = vel[:, z, rows - 1, :]
@@ -128,6 +140,8 @@
         packed = put(visc[z], nv + z, packed)
     ys[0], ys[1] = packed
 
+    loads[5].wait()
+    loads[6].wait()
     block = [dirs[pl.ds(r, probes, stride=mrows), :] for r in range(mrows)]
     rim = jnp.concatenate([stiff[...], jnp.zeros((8 - mrows, mcols), F32)], 0)
     for side, first in ((0, 0), (1, mrows - 2)):
@@ -182,9 +196,14 @@
 
     span = 2 * mcols
     pairs = mrows // 2
+    for i in (2, 3, 4):
+        loads[i].wait()
     cells = cell[...]
     low = lax.rem(cells, span)
-    group = own[...] * pairs + lax.div(cells, span)
+    owners = own[...]
+    group = jnp.where(
+        lax.rem(owners, nl) == il, lax.div(owners, nl) * pairs + lax.div(cells, span), -1
+    )
     number = lax.broadcasted_iota(jnp.int32, (span, cols), 0)
     for x in range(rows):
         onehot[:, x * cols:(x + 1) * cols] = jnp.where(
@@ -213,6 +232,9 @@
         return tuple(
             jnp.broadcast_to(xh[s, pl.ds(index, 1), :], (rows, cols)) for s in sides
         )
+
+    def image_copy(z):
+        return pltpu.make_async_copy(img.at[:, z], img_out.at[:, z], store.at[z])
 
     def plane(z, trace):
         lanes = (yh[0], yh[1])
@@ -247,113 +269,131 @@
             return carry
 
         lax.fori_loop(0, probes, probe, 0, unroll=4)
+        image_copy(z).start()
 
     for s in sides:
         arrive(near_x[s], functools.partial(x_copy, 1 - s))
         arrive(near_y[s], functools.partial(y_copy, 1 - s))
 
-    chunk = min(8, no)
+    def smooth():
+        for s in sides:
+            arrive(near_x[s], functools.partial(r_copy, 1 - s))
+        for dx, do in corners:
+            arrive(has(dx, do), functools.partial(c_copy, -dx, -do))
+
+        def edge(dx, r):
+            left, right = ch[corner_slot(dx, -1), 0:8, :], ch[corner_slot(dx, 1), 0:8, :]
+            halfs = []
+            for h in range(halves):
+                k = 2 * (r * halves + h)
+                from_right = pltpu.roll(right, mcols - k, 1) if k else right
+                from_left = pltpu.roll(left, mcols - 2 - k, 1)
+                halfs.append(
+                    jnp.where(lane < 2, from_right, jnp.where(lane >= mcols - 2, from_left, 0.0))
+                )
+            return jnp.concatenate(halfs, 0)
+
+        wide = {}
+        for r in range(2):
+            wide[r - 2] = jnp.concatenate(
+                [rh[0, r * probes:(r + 1) * probes, :], edge(-1, mrows - 2 + r)], 1
+            )
+            wide[mrows + r] = jnp.concatenate(
+                [rh[1, r * probes:(r + 1) * probes, :], edge(1, r)], 1
+            )
+        for r in range(mrows):
+            wide[r] = jnp.concatenate([dirs[pl.ds(r, probes, stride=mrows), :], edge(0, r)], 1)
+
+        def laplace(field, r):
+            return (
+                4.0 * field[r] - field[r - 1] - field[r + 1]
+                - pltpu.roll(field[r], 1, 1) - pltpu.roll(field[r], 2 * mcols - 1, 1)
+            )
+
+        line = lax.broadcasted_iota(jnp.int32, (1, mcols), 1)
+        inner = {}
+        for r in range(-1, mrows + 1):
+            if r < 0:
+                soft = rh[0, 2 * probes + mrows - 1:2 * probes + mrows, :]
+            elif r == mrows:
+                soft = rh[1, 2 * probes:2 * probes + 1, :]
+            else:
+                soft = stiff[r:r + 1, :]
+            outer = jnp.zeros((1, mcols), F32)
+            if 0 <= r < mrows:
+                outer = jnp.where(
+                    line == 0, ch[corner_slot(0, 1), 8 + r:9 + r, :],
+                    jnp.where(line == mcols - 1, ch[corner_slot(0, -1), 8 + r:9 + r, :], 0.0),
+                )
+            inner[r] = jnp.concatenate([soft, outer], 1) * laplace(wide, r)
+        for r in range(mrows):
+            prior[r * probes:(r + 1) * probes, :] = (
+                laplace(inner, r) + 0.1 * wide[r]
+            )[:, :mcols]
+
+    chunk = min(8, ny)
     tall = 2 * probes
 
-    def part_copy(owner):
+    def trace_copy(layer):
         return remote(
-            part.at[owner], got.at[iy], part_send.at[owner], part_recv.at[iy], place(ix, owner)
+            tr, tr, trace_send.at[layer], trace_recv, (ix, iy, layer)
+        )
+
+    def part_copy(to):
+        return remote(
+            part.at[to], got.at[iy], part_send.at[to], part_recv.at[iy], (ix, to, il)
         )
 
     @pl.when(il == 0)
     def _():
         plane(0, True)
-        coarse, fine = [], []
-        for x in range(rows):
-            values = tr[x * probes:(x + 1) * probes, :]
-            coarse.append(values.astype(BF16).astype(F32))
-            fine.append(values - coarse[-1])
-
-        def owners(base):
-            for g in range(chunk * pairs):
-                for x in range(rows):
-                    mine = group[x:x + 1, :] == base * pairs + g
-                    lhs[g * tall:(g + 1) * tall, x * cols:(x + 1) * cols] = jnp.concatenate(
-                        [jnp.where(mine, coarse[x], 0.0), jnp.where(mine, fine[x], 0.0)], 0
-                    ).astype(BF16)
-            sums = lax.dot_general(
-                lhs[...], onehot[...], (((1,), (1,)), ((), ())), preferred_element_type=F32
-            )
-            for j in range(chunk):
-                for h in range(pairs):
-                    at = (j * pairs + h) * tall
-                    both = sums[at:at + probes] + sums[at + probes:at + tall]
-                    for k in range(2):
-                        row = (2 * h + k) * probes
-                        part[base + j, row:row + probes, :] = both[:, k * mcols:(k + 1) * mcols]
-            for j in range(chunk):
-                @pl.when(base + j != me)
-                def _(j=j):
-                    part_copy(base + j).start()
-
-        if no == chunk:
-            owners(0)
-        else:
-            def step(i, carry):
-                owners(i * chunk)
-                return carry
-
-            lax.fori_loop(0, no // chunk, step, 0)
-
-    for s in sides:
-        arrive(near_x[s], functools.partial(r_copy, 1 - s))
-    for dx, do in corners:
-        arrive(has(dx, do), functools.partial(c_copy, -dx, -do))
-
-    def edge(dx, r):
-        left, right = ch[corner_slot(dx, -1), 0:8, :], ch[corner_slot(dx, 1), 0:8, :]
-        halfs = []
-        for h in range(halves):
-            k = 2 * (r * halves + h)
-            from_right = pltpu.roll(right, mcols - k, 1) if k else right
-            from_left = pltpu.roll(left, mcols - 2 - k, 1)
-            halfs.append(
-                jnp.where(lane < 2, from_right, jnp.where(lane >= mcols - 2, from_left, 0.0))
-            )
-        return jnp.concatenate(halfs, 0)
-
-    wide = {}
-    for r in range(2):
-        wide[r - 2] = jnp.concatenate(
-            [rh[0, r * probes:(r + 1) * probes, :], edge(-1, mrows - 2 + r)], 1
-        )
-        wide[mrows + r] = jnp.concatenate(
-            [rh[1, r * probes:(r + 1) * probes, :], edge(1, r)], 1
-        )
-    for r in range(mrows):
-        wide[r] = jnp.concatenate([dirs[pl.ds(r, probes, stride=mrows), :], edge(0, r)], 1)
-
-    def laplace(field, r):
-        return (
-            4.0 * field[r] - field[r - 1] - field[r + 1]
-            - pltpu.roll(field[r], 1, 1) - pltpu.roll(field[r], 2 * mcols - 1, 1)
-        )
-
-    line = lax.broadcasted_iota(jnp.int32, (1, mcols), 1)
-    inner = {}
-    for r in range(-1, mrows + 1):
-        if r < 0:
-            soft = rh[0, 2 * probes + mrows - 1:2 * probes + mrows, :]
-        elif r == mrows:
-            soft = rh[1, 2 * probes:2 * probes + 1, :]
-        else:
-            soft = stiff[r:r + 1, :]
-        outer = jnp.zeros((1, mcols), F32)
-        if 0 <= r < mrows:
-            outer = jnp.where(
-                line == 0, ch[corner_slot(0, 1), 8 + r:9 + r, :],
-                jnp.where(line == mcols - 1, ch[corner_slot(0, -1), 8 + r:9 + r, :], 0.0),
-            )
-        inner[r] = jnp.concatenate([soft, outer], 1) * laplace(wide, r)
-    for r in range(mrows):
-        prior[r * probes:(r + 1) * probes, :] = (
-            laplace(inner, r) + 0.1 * wide[r]
-        )[:, :mcols]
+        for layer in range(1, nl):
+            trace_copy(layer).start()
+
+    @pl.when(il != 0)
+    def _():
+        smooth()
+        trace_copy(0).wait_recv()
+
+    coarse, fine = [], []
+    for x in range(rows):
+        values = tr[x * probes:(x + 1) * probes, :]
+        coarse.append(values.astype(BF16).astype(F32))
+        fine.append(values - coarse[-1])
+
+    def reduce_chunk(base):
+        for g in range(chunk * pairs):
+            for x in range(rows):
+                mine = group[x:x + 1, :] == base * pairs + g
+                lhs[g * tall:(g + 1) * tall, x * cols:(x + 1) * cols] = jnp.concatenate(
+                    [jnp.where(mine, coarse[x], 0.0), jnp.where(mine, fine[x], 0.0)], 0
+                ).astype(BF16)
+        sums = lax.dot_general(
+            lhs[...], onehot[...], (((1,), (1,)), ((), ())), preferred_element_type=F32
+        )
+        for j in range(chunk):
+            for h in range(pairs):
+                at = (j * pairs + h) * tall
+                both = sums[at:at + probes] + sums[at + probes:at + tall]
+                for k in range(2):
+                    row = (2 * h + k) * probes
+                    part[base + j, row:row + probes, :] = both[:, k * mcols:(k + 1) * mcols]
+
+    if ny == chunk:
+        reduce_chunk(0)
+    else:
+        def chunk_step(i, carry):
+            reduce_chunk(i * chunk)
+            return carry
+
+        lax.fori_loop(0, ny // chunk, chunk_step, 0)
+    steps = sorted(range(1, ny), key=lambda step: abs(step - ny // 2))
+    for step in steps:
+        part_copy(lax.rem(iy + step, ny)).start()
+
+    @pl.when(il == 0)
+    def _():
+        smooth()
 
     for s in sides:
         arrive(near_l[s], functools.partial(m_copy, 1 - s))
@@ -366,22 +406,19 @@
     for z in range(1, depth):
         plane(z, False)
 
-    for b in range(ny):
-        at_home = jnp.logical_and(il == 0, iy == b)
-
-        @pl.when(at_home)
-        def _():
-            prior[...] += part[me]
-
-        @pl.when(jnp.logical_not(at_home))
-        def _(b=b):
-            remote(
-                part.at[0], got.at[b], part_send.at[0], part_recv.at[b], place(ix, me)
-            ).wait_recv()
-            prior[...] += got[b]
-
+    for step in reversed(steps):
+        b = lax.rem(iy + step, ny)
+        remote(
+            part.at[0], got.at[b], part_send.at[0], part_recv.at[b], (ix, b, il)
+        ).wait_recv()
     for r in range(mrows):
-        hess[pl.ds(r, probes, stride=mrows), :] = prior[r * probes:(r + 1) * probes, :]
+        at = slice(r * probes, (r + 1) * probes)
+        total = prior[at, :] + part[iy, at, :]
+        for step in range(1, ny):
+            total = total + got[lax.rem(iy + step, ny), at, :]
+        hess[pl.ds(r, probes, stride=mrows), :] = total
+    hess_copy = pltpu.make_async_copy(hess, hess_out, store.at[depth])
+    hess_copy.start()
 
     def sent(near, copy):
         @pl.when(near)
@@ -396,8 +433,38 @@
             sent(near, functools.partial(copy, s))
     for dx, do in corners:
         sent(has(dx, do), functools.partial(c_copy, dx, do))
-    for owner in range(no):
-        sent(jnp.logical_and(il == 0, me != owner), functools.partial(part_copy, owner))
+    for step in steps:
+        part_copy(lax.rem(iy + step, ny)).wait_send()
+    for layer in range(1, nl):
+        sent(il == 0, functools.partial(trace_copy, layer))
+    for z in range(depth):
+        image_copy(z).wait()
+    hess_copy.wait()
+
+
+def deliver_kernel(image, hessian, image_out, hessian_out, sems):
+    quarter = image.shape[0] // 4
+    copies = [pltpu.make_async_copy(hessian, hessian_out, sems.at[4])]
+    for i in range(4):
+        rows = pl.ds(i * quarter, quarter)
+        copies.append(pltpu.make_async_copy(image.at[rows], image_out.at[rows], sems.at[i]))
+    for copy in copies:
+        copy.start()
+    for copy in copies:
+        copy.wait()
+
+
+def deliver(image, hessian):
+    whole = pl.BlockSpec(memory_space=pltpu.HBM)
+    return pl.pallas_call(
+        deliver_kernel,
+        out_shape=tuple(jax.ShapeDtypeStruct(a.shape, a.dtype) for a in (image, hessian)),
+        in_specs=[whole, whole],
+        out_specs=(whole, whole),
+        scratch_shapes=[pltpu.SemaphoreType.DMA((5,))],
+        compiler_params=pltpu.CompilerParams(vmem_limit_bytes=60 << 20),
+        name="deliver",
+    )(image, hessian)
 
 
 def shards(velocity, viscosity, friction, owner, cell, directions, stiffness):
@@ -405,20 +472,28 @@
     depth, rows, cols = viscosity.shape
     mrows, mcols = stiffness.shape
     counts = tuple(lax.axis_size(axis) for axis in ("mapx", "mapy", "layer"))
-    no = counts[1] * counts[2]
     nq = probes * 2
     nv = nq * depth
-    chunk = min(8, no)
-    vmem = pl.BlockSpec(memory_space=pltpu.VMEM)
+    chunk = min(8, counts[1])
+    whole = pl.BlockSpec(memory_space=pltpu.HBM)
     image, hessian = pl.pallas_call(
         functools.partial(kernel, counts),
         out_shape=(
             jax.ShapeDtypeStruct((nq, depth, rows, cols), F32),
             jax.ShapeDtypeStruct((probes * mrows, mcols), F32),
         ),
-        in_specs=[vmem] * 7,
-        out_specs=(vmem, vmem),
+        in_specs=[whole] * 7,
+        out_specs=(whole, whole),
         scratch_shapes=[
+            pltpu.VMEM((nq, depth, rows, cols), F32),
+            pltpu.VMEM((depth, rows, cols), F32),
+            pltpu.VMEM((rows, cols), F32),
+            pltpu.VMEM((rows, cols), jnp.int32),
+            pltpu.VMEM((rows, cols), jnp.int32),
+            pltpu.VMEM((probes * mrows, mcols), F32),
+            pltpu.VMEM((mrows, mcols), F32),
+            pltpu.VMEM((nq, depth, rows, cols), F32),
+            pltpu.VMEM((probes * mrows, mcols), F32),
             pltpu.VMEM((2, nv + 8, cols), F32),
             pltpu.VMEM((2, nv + 8, cols), F32),
             pltpu.VMEM((2, rows, cols), F32),
@@ -432,16 +507,20 @@
             pltpu.VMEM((rows * probes, cols), F32),
             pltpu.VMEM((2 * mcols, rows * cols), BF16),
             pltpu.VMEM((chunk * (mrows // 2) * 2 * probes, rows * cols), BF16),
-            pltpu.VMEM((no, mrows * probes, mcols), F32),
+            pltpu.VMEM((counts[1], mrows * probes, mcols), F32),
             pltpu.VMEM((counts[1], mrows * probes, mcols), F32),
             pltpu.VMEM((mrows * probes, mcols), F32),
+            pltpu.SemaphoreType.DMA((7,)),
+            pltpu.SemaphoreType.DMA((depth + 1,)),
             pltpu.SemaphoreType.DMA((16,)),
             pltpu.SemaphoreType.DMA((16,)),
-            pltpu.SemaphoreType.DMA((no,)),
             pltpu.SemaphoreType.DMA((counts[1],)),
+            pltpu.SemaphoreType.DMA((counts[1],)),
+            pltpu.SemaphoreType.DMA((counts[2],)),
+            pltpu.SemaphoreType.DMA,
         ],
         compiler_params=pltpu.CompilerParams(
-            collective_id=0, has_side_effects=True, vmem_limit_bytes=32 << 20
+            collective_id=0, has_side_effects=True, vmem_limit_bytes=60 << 20
         ),
         name="hessian_action",
     )(
@@ -453,6 +532,7 @@
         directions.reshape(probes * mrows, mcols),
         stiffness,
     )
+    image, hessian = deliver(image, hessian)
     return image.reshape(velocity.shape), hessian.reshape(directions.shape)
 
 

time: 22.8 us -> 27.5 us (1.21)
  the two profiles are of different devices: /device:TPU:0 before, /device:TPU:4 now
where the time goes in v2:
time: 27.5 us; the launch traced here: 27.3 us
  Pallas kernels  26.6 us (97%)
  between operations  0.64 us (2%)
    pallas_call x1, Pallas kernels, shards(): pl.pallas_call(functools.partial(kernel, counts), out_shape=(jax.ShapeDty...  16.5 us
    pallas_call x1, Pallas kernels, deliver(): pl.pallas_call(deliver_kernel, out_shape=tuple((jax.ShapeDtypeStruct(a.sh...  10.1 us

profile of v2, /device:TPU:4, one launch (start us, length us, event | category | flops | bytes accessed | tf_op | source)
XLA Modules:
  0.0 27.3 jit_solution(17610095510744180643)
XLA Ops:
  0.6 16.5 %hessian_action.1 = (f32[32,2,8,128]{3,2,1,0:T(8,128)}, f32[64,128]{1,0:T(8,128)}) custom-call(f32[32,2,8,128]{3,2,1,0:T(8,128)} %bitcast.6, f32[2,8,128]{2,1,0:T(8,128)} %refs_1_.1, f32[8,128]{1,0:T(8,128)} %refs_2_.1, s32[8,128]{1,0:T(8,128)} %bitcast.8, s32[8,128]{1,0:T(8,128)} %bitcast.9, f32[64,128]{1,0:T(8,128)} %bitcast.7, f32[4,128]{1,0:T(4,128)} %refs_6_.1), custom_call_target="tpu_custom_call" | custom-call | tf_op jit(solution)/shard_map/hessian_action/pallas_call | solution.py:479
  17.2 10.1 %deliver.1 = (f32[32,2,8,128]{3,2,1,0:T(8,128)}, f32[64,128]{1,0:T(8,128)}) custom-call(f32[32,2,8,128]{3,2,1,0:T(8,128)} %get-tuple-element.6.image, f32[64,128]{1,0:T(8,128)} %get-tuple-element.7.hessian), custom_call_target="tpu_custom_call" | custom-call | tf_op jit(solution)/shard_map/deliver/pallas_call | solution.py:459

commit v3 on v2

--- a/solution.py
+++ b/solution.py
@@ -57,14 +57,13 @@
         return good_x if good_o is None else jnp.logical_and(good_x, good_o)
 
     barrier = pltpu.get_barrier_semaphore()
-    for step in range(1, no):
-        other = lax.rem(me + step, no)
-        pl.semaphore_signal(
-            barrier, inc=1, device_id=place(ix, other), device_id_type=pl.DeviceIdType.MESH
-        )
-    greeted = no - 1
-    for dx in (-1, 1):
-        for do in (-1, 0, 1):
+    for step in range(1, ny):
+        pl.semaphore_signal(barrier, inc=1, device_id=(ix, lax.rem(iy + step, ny), il), device_id_type=pl.DeviceIdType.MESH)
+    for step in range(1, nl):
+        pl.semaphore_signal(barrier, inc=1, device_id=(ix, iy, lax.rem(il + step, nl)), device_id_type=pl.DeviceIdType.MESH)
+    greeted = ny - 1 + nl - 1
+    for dx in (-1, 0, 1):
+        for do in ((-1, 1) if dx == 0 else (-1, 0, 1)):
             near = has(dx, do)
             greeted = greeted + near.astype(jnp.int32)
 
@@ -331,6 +330,11 @@
                 laplace(inner, r) + 0.1 * wide[r]
             )[:, :mcols]
 
+    def arrive_layers():
+        for s in reversed(sides):
+            arrive(near_l[s], functools.partial(m_copy, 1 - s))
+            arrive(near_l[s], functools.partial(z_copy, 1 - s))
+
     chunk = min(8, ny)
     tall = 2 * probes
 
@@ -353,6 +357,9 @@
     @pl.when(il != 0)
     def _():
         smooth()
+        arrive_layers()
+        for z in reversed(range(depth)):
+            plane(z, False)
         trace_copy(0).wait_recv()
 
     coarse, fine = [], []
@@ -394,17 +401,9 @@
     @pl.when(il == 0)
     def _():
         smooth()
-
-    for s in sides:
-        arrive(near_l[s], functools.partial(m_copy, 1 - s))
-        arrive(near_l[s], functools.partial(z_copy, 1 - s))
-
-    @pl.when(il != 0)
-    def _():
-        plane(0, False)
-
-    for z in range(1, depth):
-        plane(z, False)
+        arrive_layers()
+        for z in range(1, depth):
+            plane(z, False)
 
     for step in reversed(steps):
         b = lax.rem(iy + step, ny)
@@ -442,15 +441,24 @@
     hess_copy.wait()
 
 
-def deliver_kernel(image, hessian, image_out, hessian_out, sems):
+def deliver_kernel(image, hessian, image_out, hessian_out, image_in, hessian_in, first, second):
     quarter = image.shape[0] // 4
-    copies = [pltpu.make_async_copy(hessian, hessian_out, sems.at[4])]
+    steps = [(hessian, hessian_in, hessian_out)]
     for i in range(4):
         rows = pl.ds(i * quarter, quarter)
-        copies.append(pltpu.make_async_copy(image.at[rows], image_out.at[rows], sems.at[i]))
-    for copy in copies:
+        steps.append((image.at[rows], image_in.at[rows], image_out.at[rows]))
+    loads = [
+        pltpu.make_async_copy(src, mid, first.at[i]) for i, (src, mid, _) in enumerate(steps)
+    ]
+    stores = [
+        pltpu.make_async_copy(mid, dst, second.at[i]) for i, (_, mid, dst) in enumerate(steps)
+    ]
+    for copy in loads:
         copy.start()
-    for copy in copies:
+    for load, store in zip(loads, stores):
+        load.wait()
+        store.start()
+    for copy in stores:
         copy.wait()
 
 
@@ -461,7 +469,12 @@
         out_shape=tuple(jax.ShapeDtypeStruct(a.shape, a.dtype) for a in (image, hessian)),
         in_specs=[whole, whole],
         out_specs=(whole, whole),
-        scratch_shapes=[pltpu.SemaphoreType.DMA((5,))],
+        scratch_shapes=[
+            pltpu.VMEM(image.shape, F32),
+            pltpu.VMEM(hessian.shape, F32),
+            pltpu.SemaphoreType.DMA((5,)),
+            pltpu.SemaphoreType.DMA((5,)),
+        ],
         compiler_params=pltpu.CompilerParams(vmem_limit_bytes=60 << 20),
         name="deliver",
     )(image, hessian)

time: 27.5 us -> 18.9 us (0.69)
  Pallas kernels: 26.6 us -> 18.1 us
    pallas_call x1, Pallas kernels: 10.1 us -> 1.67 us  [deliver(): pl.pallas_call(deliver_kernel, out_shape=tuple((jax.ShapeDtypeStruct(a.sh...]
where the time goes in v3:
time: 18.9 us; the launch traced here: 18.7 us
  Pallas kernels  18.1 us (96%)
  between operations  0.64 us (3%)
    pallas_call x1, Pallas kernels, shards(): pl.pallas_call(functools.partial(kernel, counts), out_shape=(jax.ShapeDty...  16.4 us
    pallas_call x1, Pallas kernels, deliver(): pl.pallas_call(deliver_kernel, out_shape=tuple((jax.ShapeDtypeStruct(a.sh...  1.67 us

profile of v3, /device:TPU:4, one launch (start us, length us, event | category | flops | bytes accessed | tf_op | source)
XLA Modules:
  0.0 18.7 jit_solution(12465138876748303794)
XLA Ops:
  0.6 16.4 %hessian_action.1 = (f32[32,2,8,128]{3,2,1,0:T(8,128)}, f32[64,128]{1,0:T(8,128)}) custom-call(f32[32,2,8,128]{3,2,1,0:T(8,128)} %bitcast.6, f32[2,8,128]{2,1,0:T(8,128)} %refs_1_.1, f32[8,128]{1,0:T(8,128)} %refs_2_.1, s32[8,128]{1,0:T(8,128)} %bitcast.8, s32[8,128]{1,0:T(8,128)} %bitcast.9, f32[64,128]{1,0:T(8,128)} %bitcast.7, f32[4,128]{1,0:T(4,128)} %refs_6_.1), custom_call_target="tpu_custom_call" | custom-call | tf_op jit(solution)/shard_map/hessian_action/pallas_call | solution.py:492
  17.0 1.7 %deliver.1 = (f32[32,2,8,128]{3,2,1,0:T(8,128)}, f32[64,128]{1,0:T(8,128)}) custom-call(f32[32,2,8,128]{3,2,1,0:T(8,128)} %get-tuple-element.6.image, f32[64,128]{1,0:T(8,128)} %get-tuple-element.7.hessian), custom_call_target="tpu_custom_call" | custom-call | tf_op jit(solution)/shard_map/deliver/pallas_call | solution.py:467

commit v4 on v3

--- a/solution.py
+++ b/solution.py
@@ -28,8 +28,6 @@
         pltpu.make_async_copy(src, dst, load.at[i])
         for i, (src, dst) in enumerate(zip(inputs, staged))
     ]
-    for copy in loads:
-        copy.start()
     vel, visc, fric, own, cell, dirs, stiff = staged
     nx, ny, nl = counts
     no = ny * nl
@@ -65,6 +63,8 @@
     for dx in (-1, 0, 1):
         for do in ((-1, 1) if dx == 0 else (-1, 0, 1)):
             near = has(dx, do)
+            if dx == 0:
+                near = jnp.logical_and(near, il == (0 if do < 0 else nl - 1))
             greeted = greeted + near.astype(jnp.int32)
 
             @pl.when(near)
@@ -73,6 +73,9 @@
                     barrier, inc=1, device_id=place(ix + dx, me + do),
                     device_id_type=pl.DeviceIdType.MESH,
                 )
+
+    for copy in loads:
+        copy.start()
 
     def remote(src, dst, out_sem, in_sem, device):
         return pltpu.make_async_remote_copy(
@@ -172,12 +175,12 @@
         when_near(near_x[s], functools.partial(x_copy, s))
         when_near(near_y[s], functools.partial(y_copy, s))
     for s in sides:
-        when_near(near_l[s], functools.partial(m_copy, s))
-        when_near(near_l[s], functools.partial(z_copy, s))
-    for s in sides:
         when_near(near_x[s], functools.partial(r_copy, s))
     for dx, do in corners:
         when_near(has(dx, do), functools.partial(c_copy, dx, do))
+    for s in sides:
+        when_near(near_l[s], functools.partial(m_copy, s))
+        when_near(near_l[s], functools.partial(z_copy, s))
 
     def zero_unless(near, ref, at):
         @pl.when(jnp.logical_not(near))

time: 18.9 us -> 18.8 us (level)
  no operation moved by 1% of the time
where the time goes in v4:
time: 18.8 us; the launch traced here: 18.7 us
  Pallas kernels  18 us (96%)
  between operations  0.64 us (3%)
    pallas_call x1, Pallas kernels, shards(): pl.pallas_call(functools.partial(kernel, counts), out_shape=(jax.ShapeDty...  16.3 us
    pallas_call x1, Pallas kernels, deliver(): pl.pallas_call(deliver_kernel, out_shape=tuple((jax.ShapeDtypeStruct(a.sh...  1.67 us

profile of v4, /device:TPU:4, one launch (start us, length us, event | category | flops | bytes accessed | tf_op | source)
XLA Modules:
  0.0 18.7 jit_solution(7617685148767784319)
XLA Ops:
  0.6 16.3 %hessian_action.1 = (f32[32,2,8,128]{3,2,1,0:T(8,128)}, f32[64,128]{1,0:T(8,128)}) custom-call(f32[32,2,8,128]{3,2,1,0:T(8,128)} %bitcast.6, f32[2,8,128]{2,1,0:T(8,128)} %refs_1_.1, f32[8,128]{1,0:T(8,128)} %refs_2_.1, s32[8,128]{1,0:T(8,128)} %bitcast.8, s32[8,128]{1,0:T(8,128)} %bitcast.9, f32[64,128]{1,0:T(8,128)} %bitcast.7, f32[4,128]{1,0:T(4,128)} %refs_6_.1), custom_call_target="tpu_custom_call" | custom-call | tf_op jit(solution)/shard_map/hessian_action/pallas_call | solution.py:495
  17.0 1.7 %deliver.1 = (f32[32,2,8,128]{3,2,1,0:T(8,128)}, f32[64,128]{1,0:T(8,128)}) custom-call(f32[32,2,8,128]{3,2,1,0:T(8,128)} %get-tuple-element.6.image, f32[64,128]{1,0:T(8,128)} %get-tuple-element.7.hessian), custom_call_target="tpu_custom_call" | custom-call | tf_op jit(solution)/shard_map/deliver/pallas_call | solution.py:470
